TPU v7x, 32 devices: a whole 2x2x4 slice. The times are simulated.
32 devices in a mesh: dp: 8 (over z, core), expert: 4 (over y, x).
Axes of the slice: x: 2, y: 2, z: 4, core: 2. Of those that a mesh axis runs over, the one named last changes fastest.
Arguments:
- features: bfloat16 [1024, 1024], P('dp'), may hold values from -6 to 6
- cross_weight: bfloat16 [1, 1024, 1024], replicated, may hold values from -0.1875 to 0.1875
- cross_bias: float32 [1, 1024], replicated, may hold values from -3 to 3
- gate_weight: bfloat16 [1024, 64], replicated, may hold values from -0.1875 to 0.1875
- gate_offset: float32 [64], replicated, may hold values from -3 to 3
- up_weight: bfloat16 [16, 1024, 8192], P('expert', None, 'dp'), may hold values from -0.1875 to 0.1875
- down_weight: bfloat16 [16, 8192, 1024], P('expert', 'dp'), may hold values from -0.0625 to 0.0625
- task_grad: bfloat16 [1024, 4, 1024], P('dp'), may hold values from -6 to 6
Outputs:
- task_mixed: bfloat16 [1024, 4, 1024], P('dp')
- feature_grad: bfloat16 [1024, 1024], P('dp')
- up_grad: bfloat16 [16, 1024, 8192], P('expert', None, 'dp')
- down_grad: bfloat16 [16, 8192, 1024], P('expert', 'dp')
- cross_grad: float32 [1, 1024, 1024], replicated
- bias_grad: float32 [1, 1024], replicated
- gating_grad: float32 [1024, 64], replicated
- offset_grad: float32 [64], replicated
All inputs are finite; a program needn't handle non-finite values.
Results may differ from a plain program's by a relative error of at most 0.012.
Values may be sent and summed in bfloat16 or wider, within the bound.
No kernel may reach another device: no remote copies, remote signals or barrier semaphores. Data moves between devices by JAX's collectives and lax.ppermute only.
A program may use at most 192 MiB of HBM per device.

v0:
```python
import jax
import jax.numpy as jnp
from jax import lax
from jax.sharding import PartitionSpec as P


def cross_forward(features, cross_weight, cross_bias):
    states = features.astype(jnp.float32)
    low = states.astype(jnp.bfloat16)
    update = jnp.dot(low, cross_weight[0], preferred_element_type=jnp.float32) + cross_bias[0]
    states = features.astype(jnp.float32) * update + states
    rounded = [low]
    updates = [update]
    return (states, rounded, updates)


def cross_backward(features, cross_weight, rounded, updates, upstream):
    base = features.astype(jnp.float32)
    direct = jnp.zeros_like(upstream)
    weight_terms = []
    bias_terms = []
    for layer in reversed(range(len(rounded))):
        scaled = (upstream * base).astype(jnp.bfloat16)
        weight_terms.insert(
            0, jnp.dot(rounded[layer].T, scaled, preferred_element_type=jnp.float32)
        )
        bias_terms.insert(0, jnp.sum(scaled.astype(jnp.float32), axis=0))
        direct = upstream * updates[layer]
        upstream = upstream + jnp.dot(
            scaled, cross_weight[layer].T, preferred_element_type=jnp.float32
        )
    return (
        (upstream + direct).astype(jnp.bfloat16),
        jnp.stack(weight_terms),
        jnp.stack(bias_terms),
    )


def gating(shared, gate_weight, gate_offset, tasks):
    logits = jnp.dot(shared, gate_weight, preferred_element_type=jnp.float32) + gate_offset
    logits = logits.reshape(shared.shape[0], tasks, gate_weight.shape[1] // tasks)
    expo = jnp.exp(logits)
    return expo / jnp.sum(expo, axis=-1, keepdims=True)


def spread_grad(gate_probs, task_rows):
    total = gate_probs[:, 0, :, None] * task_rows[:, 0, None, :].astype(jnp.float32)
    for task in range(1, task_rows.shape[1]):
        total = total + gate_probs[:, task, :, None] * task_rows[:, task, None, :].astype(
            jnp.float32
        )
    return total.astype(jnp.bfloat16)


def task_inner(task_rows, expert_rows):
    columns = []
    for task in range(task_rows.shape[1]):
        columns.append(
            jnp.sum(task_rows[:, task, None, :].astype(jnp.float32) * expert_rows, axis=-1)
        )
    return jnp.stack(columns, axis=1)


def local(
    features, cross_weight, cross_bias, gate_weight, gate_offset, up_weight, down_weight, task_grad
):
    tasks = task_grad.shape[1]
    exp_dev = up_weight.shape[0]
    high = lax.Precision.HIGHEST
    states, rounded, updates = cross_forward(features, cross_weight, cross_bias)
    shared = states.astype(jnp.bfloat16)
    gate_probs = gating(shared, gate_weight, gate_offset, tasks)
    first_expert = lax.axis_index("expert") * exp_dev
    gates_local = lax.dynamic_slice_in_dim(gate_probs, first_expert, exp_dev, 2)
    everyone = lax.all_gather(shared, "dp", axis=0, tiled=True)
    hidden_pre = jnp.einsum("rd,edh->reh", everyone, up_weight, preferred_element_type=jnp.float32)
    sig = jax.nn.sigmoid(hidden_pre)
    hidden_act = (hidden_pre * sig).astype(jnp.bfloat16)
    group_out = lax.psum_scatter(
        jnp.einsum("reh,ehd->red", hidden_act, down_weight, preferred_element_type=jnp.float32),
        "dp",
        scatter_dimension=0,
        tiled=True,
    )
    all_out = lax.all_gather(group_out, "expert", axis=1, tiled=True)
    mixed_wide = jnp.einsum("rte,red->rtd", gate_probs, all_out, precision=high)
    gate_grad = task_inner(task_grad, all_out)
    task_mixed = mixed_wide.astype(jnp.bfloat16)
    own_grad = spread_grad(gates_local, task_grad)
    out_grad = lax.all_gather(own_grad, "dp", axis=0, tiled=True)
    logit_grad = gate_probs * (gate_grad - jnp.sum(gate_probs * gate_grad, axis=-1, keepdims=True))
    logit_flat = logit_grad.reshape(shared.shape[0], gate_weight.shape[1])
    logit_low = logit_flat.astype(jnp.bfloat16)
    hidden_grad = jnp.einsum(
        "red,ehd->reh", out_grad, down_weight, preferred_element_type=jnp.float32
    )
    pre_grad = (hidden_grad * sig * (1.0 + hidden_pre * (1.0 - sig))).astype(jnp.bfloat16)
    down_grad = jnp.einsum(
        "reh,red->ehd", hidden_act, out_grad, preferred_element_type=jnp.float32
    ).astype(jnp.bfloat16)
    up_grad = jnp.einsum(
        "rd,reh->edh", everyone, pre_grad, preferred_element_type=jnp.float32
    ).astype(jnp.bfloat16)
    group_grad = lax.psum_scatter(
        jnp.einsum("reh,edh->rd", pre_grad, up_weight, preferred_element_type=jnp.float32),
        "dp",
        scatter_dimension=0,
        tiled=True,
    )
    shared_grad = lax.psum(group_grad, "expert")
    shared_grad = shared_grad + jnp.dot(
        logit_low, gate_weight.T, preferred_element_type=jnp.float32
    )
    gating_part = jnp.dot(shared.T, logit_low, preferred_element_type=jnp.float32)
    offset_part = jnp.sum(logit_flat, axis=0)
    feature_grad, cross_part, bias_part = cross_backward(
        features, cross_weight, rounded, updates, shared_grad
    )
    cross_grad, bias_grad, gating_grad, offset_grad = lax.psum(
        (cross_part, bias_part, gating_part, offset_part), "dp"
    )
    return (
        task_mixed,
        feature_grad,
        up_grad,
        down_grad,
        cross_grad,
        bias_grad,
        gating_grad,
        offset_grad,
    )


def solution(mesh):
    placed = (
        P("dp", None),
        P(),
        P(),
        P(),
        P(),
        P("expert", None, "dp"),
        P("expert", "dp", None),
        P("dp", None, None),
    )
    return jax.shard_map(
        local,
        mesh=mesh,
        in_specs=placed,
        out_specs=(
            P("dp", None, None),
            P("dp", None),
            P("expert", None, "dp"),
            P("expert", "dp", None),
            P(),
            P(),
            P(),
            P(),
        ),
        check_vma=False,
    )
```

profile of v0, /device:TPU:0, one launch (start us, length us, event | category | flops | bytes accessed | tf_op | source)
XLA Modules:
  0.0 603.0 jit_solution(6396345517934946824)
XLA Ops:
  7.2 1.5 copy-done
  8.8 2.4 fusion.30
  13.2 4.4 fusion.43
  19.1 1.6 add_convert_fusion
  20.7 22.4 %all-gather.4.cloned.1.call-done = bf16[1024,1024]{1,0:T(8,128)(2,1)} async-done(((bf16[128,1024]{1,0:T(8,128)(2,1)}), bf16[1024,1024]{1,0:T(8,128)(2,1)}) %all-gather.4.cloned.1.call-update) | async-done | bytes 2097168 | tf_op jit(solution)/shard_map/all_gather | solution.py:75
  43.2 15.9 %fusion.6 = f32[1024,4,1024]{2,0,1:T(8,128)} fusion(bf16[4,1024,1024]{2,1,0:T(8,128)(2,1)} %param.13, bf16[1024,1024]{1,0:T(8,128)(2,1)} %all-gather.4.cloned.1.call-done), kind=kOutput, calls=%fused_computation.18 | convolution fusion | flops 8589934592 | bytes 27262976 | tf_op jit(solution)/shard_map/rd,edh->reh/dot_general | solution.py:76
  59.1 18.2 %convolution_bitcast_fusion = f32[1024,4,1024]{2,0,1:T(8,128)} fusion(bf16[4,1024,1024]{2,1,0:T(8,128)(2,1)} %param.14, f32[1024,4,1024]{2,0,1:T(8,128)} %fusion.6), kind=kOutput, calls=%fused_computation.6 | convolution fusion | flops 8610906112 | bytes 41943040 | tf_op jit(solution)/shard_map/reh,ehd->red/dot_general | solution.py:80
  77.5 49.4 %all-gather.8.cloned.1.call-done = bf16[1024,4,1024]{2,0,1:T(8,128)(2,1)} async-done(((bf16[128,4,1024]{2,0,1:T(8,128)(2,1)}), bf16[1024,4,1024]{2,0,1:T(8,128)(2,1)}) %all-gather.8.cloned.1.call-update) | async-done | bytes 8388624 | tf_op jit(solution)/shard_map/all_gather | solution.py:90
  127.0 20.5 %fusion.2 = bf16[1024,4,1024]{2,0,1:T(8,128)(2,1)} fusion(f32[1024,4,1024]{2,0,1:T(8,128)} %fusion.6, bf16[1024,4,1024]{2,0,1:T(8,128)(2,1)} %all-gather.8.cloned.1.call-done, bf16[4,1024,1024]{2,1,0:T(8,128)(2,1)} %param.14), kind=kOutput, calls=%fused_computation.3 | convolution fusion | flops 8627683328 | bytes 41943040 | tf_op jit(solution)/shard_map/red,ehd->reh/dot_general | solution.py:94
  147.5 15.1 %convolution_bitcast_fusion.2 = f32[1024,1024]{1,0:T(8,128)} fusion(bf16[1024,4,1024]{2,0,1:T(8,128)(2,1)} %fusion.2, bf16[4,1024,1024]{2,1,0:T(8,128)(2,1)} %param.13), kind=kOutput, calls=%fused_computation.16 | convolution fusion | flops 8589934592 | bytes 20971520 | tf_op jit(solution)/shard_map/reh,edh->rd/dot_general | solution.py:105
  162.7 133.4 %reduce-scatter.3.cloned.1.call-done = f32[128,4,1024]{2,0,1:T(8,128)} async-done(((f32[1024,4,1024]{2,0,1:T(8,128)}), f32[128,4,1024]{2,0,1:T(8,128)}) %reduce-scatter.3.cloned.1.call-update) | async-done | bytes 2097168 | tf_op jit(solution)/shard_map/reduce_scatter | solution.py:79
  297.3 17.0 %convolution_convert_fusion = bf16[4,1024,1024]{2,1,0:T(8,128)(2,1)} fusion(bf16[1024,4,1024]{2,0,1:T(8,128)(2,1)} %all-gather.8.cloned.1.call-done, f32[1024,4,1024]{2,0,1:T(8,128)} %fusion.6), kind=kOutput, calls=%fused_computation.14 | convolution fusion | flops 8615100416 | bytes 33554432 | tf_op jit(solution)/shard_map/reh,red->ehd/dot_general | solution.py:98
  314.2 33.0 %reduce-scatter.5.cloned.1.call-done = f32[128,1024]{1,0:T(8,128)} async-done(((f32[1024,1024]{1,0:T(8,128)}), f32[128,1024]{1,0:T(8,128)}) %reduce-scatter.5.cloned.1.call-update) | async-done | bytes 524304 | tf_op jit(solution)/shard_map/reduce_scatter | solution.py:104
  347.3 87.4 %all-gather.6.cloned.1.call-done = f32[128,16,1024]{2,0,1:T(8,128)} async-done(((f32[128,4,1024]{2,0,1:T(8,128)}), f32[128,16,1024]{2,0,1:T(8,128)}) %all-gather.6.cloned.1.call-update) | async-done | bytes 8388624 | tf_op jit(solution)/shard_map/all_gather | solution.py:85
  434.7 5.0 multiply_reduce_fusion.3
  441.0 42.0 %all-reduce.5.cloned.1.call-done = f32[128,1024]{1,0:T(8,128)} async-done(((f32[128,1024]{1,0:T(8,128)}), f32[128,1024]{1,0:T(8,128)}) %all-reduce.5.cloned.1.call-update) | async-done | bytes 524304 | tf_op jit(solution)/shard_map/psum | solution.py:110
  484.3 2.8 convolution_bitcast_fusion.1
  487.0 15.0 %convert_bitcast_fusion = bf16[4,1024,1024]{1,2,0:T(8,128)(2,1)} fusion(bf16[1024,4,1024]{2,0,1:T(8,128)(2,1)} %fusion.2, bf16[1024,1024]{1,0:T(8,128)(2,1)} %all-gather.4.cloned.1.call-done), kind=kOutput, calls=%fused_computation.9 | convolution fusion | flops 8594128896 | bytes 18874368 | tf_op jit(solution)/shard_map/rd,reh->edh/dot_general | solution.py:101
  502.0 11.4 %copy.52 = bf16[4,1024,1024]{2,1,0:T(8,128)(2,1)} copy(bf16[4,1024,1024]{1,2,0:T(8,128)(2,1)} %convert_bitcast_fusion) | data formatting | bytes 16777216
  513.4 18.7 %all-reduce = (f32[1,1024]{1,0:T(1,128)}, f32[64]{0:T(128)}) all-reduce(f32[1,1024]{1,0:T(1,128)S(1)} %bitcast.98, f32[64]{0:T(128)S(1)} %get-tuple-element.40), channel_id=1, replica_groups=mesh['dp'=8,'expert'=4] {'dp'}, use_global_device_ids=true, to_apply=%region_11.0 | all-reduce | flops 1088 | bytes 8704 | tf_op jit(solution)/shard_map/psum | solution.py:119
  532.1 1.5 fusion.24
  533.6 13.4 %fusion.12 = bf16[128,4,1024]{2,1,0:T(4,128)(2,1)} fusion(f32[128,4,16]{2,1,0:T(4,128)} %copy.44, f32[128,16,1024]{2,0,1:T(8,128)} %all-gather.6.cloned.1.call-done), kind=kOutput, calls=%fused_computation.25 | convolution fusion | flops 101187584 | bytes 9469952 | tf_op jit(solution)/shard_map/rte,red->rtd/dot_general | solution.py:86
  547.0 42.6 %all-reduce.7.cloned.1.call-done = (f32[1,1024,1024]{1,2,0:T(8,128)}, f32[1024,64]{0,1:T(8,128)}) async-done(((f32[1,1024,1024]{1,2,0:T(8,128)}, f32[1024,64]{0,1:T(8,128)}), (f32[1,1024,1024]{1,2,0:T(8,128)}, f32[1024,64]{0,1:T(8,128)})) %all-reduce.7.cloned.1.call-update) | async-done | bytes 4456464 | tf_op jit(solution)/shard_map/psum | solution.py:119
  589.6 5.4 copy.53
  (48 shorter events, 8.1 us)
Async XLA Ops:
  7.2 1.6 copy-start
  7.2 36.0 %all-gather.4.cloned.1.call-start = ((), (), s32[]{:S(2)}) async-start(), calls=%async_computation.2 | async-start | bytes 2359296 | tf_op jit(solution)/shard_map/all_gather | solution.py:75
  11.2 115.7 %all-gather.8.cloned.1.call-start = ((), (), s32[]{:S(2)}) async-start(), calls=%async_computation.5 | async-start | bytes 9437184 | tf_op jit(solution)/shard_map/all_gather | solution.py:90
  12.5 0.6 copy-start.7
  13.1 283.3 %copy-start.10 = (f32[128,4,16]{0,2,1:T(8,128)}, f32[128,4,16]{0,2,1:T(8,128)S(1)}, u32[]{:S(2)}) copy-start(f32[128,4,16]{0,2,1:T(8,128)S(1)} %bitcast_divide_fusion.1) | copy-start | bytes 98308
  18.0 0.8 copy-start.2
  18.1 1.0 copy-start.3
  20.7 275.4 %reduce-scatter.3.cloned.1.call-start = ((), (), s32[]{:S(2)}) async-start(), calls=%async_computation.3 | async-start | bytes 18874368 | tf_op jit(solution)/shard_map/reduce_scatter | solution.py:79
  77.3 269.9 %reduce-scatter.5.cloned.1.call-start = ((), (), s32[]{:S(2)}) async-start(), calls=%async_computation.6 | async-start | bytes 4718592 | tf_op jit(solution)/shard_map/reduce_scatter | solution.py:104
  162.6 272.1 %all-gather.6.cloned.1.call-start = ((), (), s32[]{:S(2)}) async-start(), calls=%async_computation.4 | async-start | bytes 10485760 | tf_op jit(solution)/shard_map/all_gather | solution.py:85
  296.2 186.8 %all-reduce.5.cloned.1.call-start = ((), (), s32[]{:S(2)}) async-start(), calls=%async_computation.7 | async-start | bytes 1048576 | tf_op jit(solution)/shard_map/psum | solution.py:110
  314.2 168.7 %copy-start.1 = (bf16[128,1024]{1,0:T(8,128)(2,1)S(1)}, bf16[128,1024]{1,0:T(8,128)(2,1)}, u32[]{:S(2)}) copy-start(bf16[128,1024]{1,0:T(8,128)(2,1)} %param.8) | copy-start | bytes 786436
  314.2 168.7 %copy-start.6 = (bf16[1024,64]{0,1:T(8,128)(2,1)S(1)}, bf16[1024,64]{0,1:T(8,128)(2,1)}, u32[]{:S(2)}) copy-start(bf16[1024,64]{0,1:T(8,128)(2,1)} %param.11) | copy-start | bytes 393220
  347.3 242.3 %all-reduce.7.cloned.1.call-start = ((), (), s32[]{:S(2)}) async-start(), calls=%async_computation.8 | async-start | bytes 8912896 | tf_op jit(solution)/shard_map/psum | solution.py:119
  434.7 5.1 copy-start.11
  434.7 5.2 copy-start.8
  434.7 5.3 copy-start.4
  502.0 30.1 %copy-start.5 = (f32[128,1024]{1,0:T(8,128)S(1)}, f32[128,1024]{1,0:T(8,128)}, u32[]{:S(2)}) copy-start(f32[128,1024]{1,0:T(8,128)} %get-tuple-element.51) | copy-start | bytes 1572868
  589.6 5.4 copy-start.9
Sparse Core Ops, SparseCore 0:
  11.4 31.7 all-gather.3
  45.4 81.5 all-gather.7
  129.3 166.7 reduce-scatter.2
  298.9 48.3 reduce-scatter.4
  348.9 85.7 all-gather.5
  437.6 45.3 all-reduce.4
  487.2 102.4 all-reduce.6
where the time goes:
time: 611 us; the launch traced here: 603 us
  waiting for transfers between devices  410 us (67%)
  matrix products  125 us (20%)
  local copies, waits for them, and re-layouts  26 us (4%)
  blocking collectives  18.7 us (3%)
  between operations  14.7 us (2%)
  other arithmetic  7.36 us (1%)
    reduce_scatter x1, waiting for transfers between devices, local(): lax.psum_scatter(jnp.einsum('reh,ehd->red', hidden_act, down_weight, pref...  133 us
    all_gather x1, waiting for transfers between devices, local(): all_out = lax.all_gather(group_out, 'expert', axis=1, tiled=True)  87.4 us
    all_gather x1, waiting for transfers between devices, local(): out_grad = lax.all_gather(own_grad, 'dp', axis=0, tiled=True)  49.4 us
    psum x1, waiting for transfers between devices, local(): lax.psum((cross_part, bias_part, gating_part, offset_part), 'dp')  42.6 us
    psum x1, waiting for transfers between devices, local(): shared_grad = lax.psum(group_grad, 'expert')  42 us
    reduce_scatter x1, waiting for transfers between devices, local(): lax.psum_scatter(jnp.einsum('reh,edh->rd', pre_grad, up_weight, preferred...  33 us
    all_gather x1, waiting for transfers between devices, local(): everyone = lax.all_gather(shared, 'dp', axis=0, tiled=True)  22.4 us
    unnamed x27, local copies, waits for them, and re-layouts  20.7 us
  transfers between devices with their start and end apart: 7, of which 7 were waited for; matrix products, arithmetic and copies ran while one was open for 24% of the time, Pallas kernels for 0%

commit v1 on v0

v1 whole, which is shorter than its diff:
```python
import functools

import jax
import jax.numpy as jnp
from jax import lax
from jax.experimental import pallas as pl
from jax.experimental.pallas import tpu as pltpu
from jax.sharding import PartitionSpec as P

F32 = jnp.float32
BF16 = jnp.bfloat16
NN = (((1,), (0,)), ((), ()))
NT = (((1,), (1,)), ((), ()))
TN = (((0,), (0,)), ((), ()))
VMEM_LIMIT = 56 * 2**20
FORWARD_PARTS = 4
WEIGHT_PARTS = 2


def mm(a, b, dims=NN):
    return lax.dot_general(a, b, dims, preferred_element_type=F32)


def exact(values, ones):
    high = values.astype(BF16)
    low = (values - high.astype(F32)).astype(BF16)
    return mm(high, ones) + mm(low, ones)


def shift(values, size):
    assert size & (size - 1) == 0
    return lax.shift_right_logical(values, jnp.int32(size.bit_length() - 1))


def group_sum(values, experts):
    n = values.shape[1]
    row = shift(lax.broadcasted_iota(jnp.int32, (n, n), 0), experts)
    lane = shift(lax.broadcasted_iota(jnp.int32, (n, n), 1), experts)
    return exact(values, jnp.where(row == lane, 1.0, 0.0).astype(BF16))


def params(flops, name):
    return dict(
        compiler_params=pltpu.CompilerParams(vmem_limit_bytes=VMEM_LIMIT),
        cost_estimate=pl.CostEstimate(flops=flops, bytes_accessed=2**22, transcendentals=0),
        name=name,
    )


def cross_kernel(experts, sub, feat_ref, cw_ref, cb_ref, gw_ref, go_ref, shared_ref, gates_ref):
    for r in range(0, feat_ref.shape[0], sub):
        part = pl.ds(r, sub)
        base = feat_ref[part, :]
        wide = base.astype(F32)
        update = mm(base, cw_ref[...]) + cb_ref[...]
        shared = (wide * update + wide).astype(BF16)
        shared_ref[part, :] = shared
        expo = jnp.exp(mm(shared, gw_ref[...]) + go_ref[...])
        gates_ref[part, :] = expo / group_sum(expo, experts)


def cross(feat, cw, cb, gw, go, tasks):
    rows, d = feat.shape
    cols = gw.shape[1]
    sub = 256
    whole = lambda i: (0, 0)
    return pl.pallas_call(
        functools.partial(cross_kernel, cols // tasks, sub),
        grid=(rows // sub,),
        in_specs=[
            pl.BlockSpec((sub, d), lambda i: (i, 0)),
            pl.BlockSpec((d, d), whole),
            pl.BlockSpec((1, d), whole),
            pl.BlockSpec((d, cols), whole),
            pl.BlockSpec((1, cols), whole),
        ],
        out_specs=[
            pl.BlockSpec((sub, d), lambda i: (i, 0)),
            pl.BlockSpec((sub, cols), lambda i: (i, 0)),
        ],
        out_shape=[
            jax.ShapeDtypeStruct((rows, d), BF16),
            jax.ShapeDtypeStruct((rows, cols), F32),
        ],
        **params(2 * rows * d * d, "cross"),
    )(feat, cw, cb, gw, go)


def forward_kernel(shared_ref, up_ref, down_ref, *refs):
    act_ref, slope_ref, out_ref = refs[-3:]
    pre = mm(shared_ref[...], up_ref[0])
    sig = jax.nn.sigmoid(pre)
    act = pre * sig
    low = act.astype(BF16)
    act_ref[0] = low
    slope_ref[0] = (sig + act * (1.0 - sig)).astype(BF16)
    out_ref[0] = mm(low, down_ref[0]).astype(BF16)


def forward(shared, up, down, begin, count, before):
    rows, d = shared.shape
    local, _, hid = up.shape
    sub = min(rows, 512)
    here = lambda e, r: (begin + e, r, 0)
    there = lambda e, r: (begin + e, 0, 0)
    wide = jax.ShapeDtypeStruct((local, rows, hid), BF16)
    return pl.pallas_call(
        forward_kernel,
        grid=(count, rows // sub),
        in_specs=[
            pl.BlockSpec((sub, d), lambda e, r: (r, 0)),
            pl.BlockSpec((1, d, hid), there),
            pl.BlockSpec((1, hid, d), there),
        ]
        + [pl.BlockSpec(memory_space=pl.ANY) for _ in before],
        out_specs=[
            pl.BlockSpec((1, sub, hid), here),
            pl.BlockSpec((1, sub, hid), here),
            pl.BlockSpec((1, sub, d), here),
        ],
        out_shape=[wide, wide, jax.ShapeDtypeStruct((local, rows, d), BF16)],
        input_output_aliases={3 + k: k for k in range(len(before))},
        **params(4 * rows * d * hid * count, "forward"),
    )(shared, up, down, *before)


def same_row(n, m, group):
    row = lax.broadcasted_iota(jnp.int32, (n, m), 0) & (group - 1)
    lane = lax.broadcasted_iota(jnp.int32, (1, m), 1) & (group - 1)
    return jnp.where(row == lane, 1.0, 0.0)


def chosen(ids_ref, order, by_task, tasks, local, experts, cols, group):
    wide = tasks * local * group
    lane = shift(lax.broadcasted_iota(jnp.int32, (1, wide), 1), group)
    task = shift(lane, local) if by_task else lane & (tasks - 1)
    expert = lane & (local - 1) if by_task else shift(lane, tasks)
    ids = jnp.zeros_like(lane) + ids_ref[order]
    for t in range(1, tasks):
        ids = jnp.where(task == t, ids_ref[order + t], ids)
    row = lax.broadcasted_iota(jnp.int32, (cols, wide), 0)
    return jnp.where(row == ids * experts + ids_ref[0] + expert, 1.0, 0.0).astype(BF16)


def stack(weights, r, group, count, width):
    return jnp.concatenate(
        [weights[r : r + group, j * width : (j + 1) * width] for j in range(count)], axis=0
    )


def mix_kernel(tasks, experts, block, begin, ids_ref, gates_ref, outs_ref, mixed_ref):
    rows, cols = gates_ref.shape
    local = outs_ref.shape[0]
    group = 256 // local
    flat = same_row(block, tasks * local * group, group)
    step = rows // block
    for k in range(step):
        at = pl.ds(k * block, block)
        order = 1 + 2 * tasks * ((begin + pl.program_id(0)) * step + k) + tasks
        weights = mm(
            gates_ref[at, :].astype(BF16),
            chosen(ids_ref, order, True, tasks, local, experts, cols, group),
        )
        weights = (weights * flat).astype(BF16)
        for r in range(0, block, group):
            part = pl.ds(k * block + r, group)
            out = jnp.concatenate([outs_ref[j, part, :] for j in range(local)], axis=0)
            both = mm(stack(weights, r, group, tasks, local * group), out).astype(BF16)
            for t in range(tasks):
                mixed_ref[t, part, :] = both[t * group : (t + 1) * group]


def mix(ids, gates, outs, n, tasks):
    local, rows, d = outs.shape
    cols = gates.shape[1]
    sub = rows // 4

    def half(begin):
        return pl.pallas_call(
            functools.partial(mix_kernel, tasks, cols // tasks, rows // n, begin),
            grid_spec=pltpu.PrefetchScalarGridSpec(
                num_scalar_prefetch=1,
                grid=(2,),
                in_specs=[
                    pl.BlockSpec((sub, cols), lambda i, f: (begin + i, 0)),
                    pl.BlockSpec((local, sub, d), lambda i, f: (0, begin + i, 0)),
                ],
                out_specs=pl.BlockSpec((tasks, sub, d), lambda i, f: (0, i, 0)),
            ),
            out_shape=jax.ShapeDtypeStruct((tasks, rows // 2, d), BF16),
            **params(2**10 * rows * d, "mix"),
        )(ids, gates, outs)

    send = half(2)
    return half(0), send


def spread_kernel(tasks, experts, places, n_grads, ids_ref, *refs):
    grads = refs[:n_grads]
    gates_ref, outs_ref, og_ref, pair_ref, rows_ref, sems = refs[n_grads:]
    i = pl.program_id(0)
    rows, cols = gates_ref.shape
    count = rows_ref.shape[1]
    block = rows // count
    local = og_ref.shape[0]
    group = 256 // local

    def fetch(step, slot, act):
        for k in range(len(places) // count):

            @pl.when(step == k)
            def _():
                for j in range(count):
                    for t, (which, *lead) in enumerate(places[k * count + j]):
                        act(
                            pltpu.make_async_copy(
                                grads[which].at[tuple(lead)],
                                rows_ref.at[slot, j, t],
                                sems.at[slot, j, t],
                            )
                        )

    @pl.when(i == 0)
    def _():
        fetch(0, 0, lambda copy: copy.start())

    fetch(i + 1, (i + 1) & 1, lambda copy: copy.start())
    flat = same_row(block, tasks * local * group, group)
    square = same_row(tasks * group, local * group, group)
    fetch(i, i & 1, lambda copy: copy.wait())
    slot = i & 1
    for k in range(count):
        order = 1 + 2 * tasks * (i * count + k)
        at = pl.ds(k * block, block)
        gates = gates_ref[at, :]
        pick = lambda by_task: chosen(
            ids_ref, order, by_task, tasks, local, experts, cols, group
        )
        weights = (mm(gates.astype(BF16), pick(False)) * flat).astype(BF16)
        inners = []
        for r in range(0, block, group):
            part = pl.ds(k * block + r, group)
            grad = jnp.concatenate(
                [rows_ref[slot, k, t, r : r + group, :] for t in range(tasks)], axis=0
            )
            out = jnp.concatenate([outs_ref[j, part, :] for j in range(local)], axis=0)
            both = mm(stack(weights, r, group, local, tasks * group), grad).astype(BF16)
            for j in range(local):
                og_ref[j, part, :] = both[j * group : (j + 1) * group]
            products = mm(grad, out, NT) * square
            inners.append(
                jnp.concatenate(
                    [products[t * group : (t + 1) * group] for t in range(tasks)], axis=1
                )
            )
        inner = jnp.concatenate(inners, axis=0)
        high = inner.astype(BF16)
        rest = (inner - high.astype(F32)).astype(BF16)
        at_column = pick(True)
        inner = mm(high, at_column, NT) + mm(rest, at_column, NT)
        logit = gates * (inner - group_sum(gates * inner, experts))
        high = logit.astype(BF16)
        rest = (logit - high.astype(F32)).astype(BF16)
        row = lax.broadcasted_iota(jnp.int32, (cols, 2 * cols), 0)
        lane = lax.broadcasted_iota(jnp.int32, (cols, 2 * cols), 1)
        one = jnp.where(lane == row, 1.0, 0.0).astype(BF16)
        two = jnp.where(lane == row + cols, 1.0, 0.0).astype(BF16)
        pair_ref[at, :] = (mm(high, one) + mm(rest, two)).astype(BF16)


def spread_grads(ids, grads, places, gates, outs, tasks):
    local, rows, d = outs.shape
    cols = gates.shape[1]
    n = len(places)
    count = 2
    block = rows // n
    sub = count * block
    every = lambda i, f: (0, i, 0)
    return pl.pallas_call(
        functools.partial(spread_kernel, tasks, cols // tasks, places, len(grads)),
        grid_spec=pltpu.PrefetchScalarGridSpec(
            num_scalar_prefetch=1,
            grid=(n // count,),
            in_specs=[pl.BlockSpec(memory_space=pl.ANY) for _ in grads]
            + [
                pl.BlockSpec((sub, cols), lambda i, f: (i, 0)),
                pl.BlockSpec((local, sub, d), every),
            ],
            out_specs=[
                pl.BlockSpec((local, sub, d), every),
                pl.BlockSpec((sub, 2 * cols), lambda i, f: (i, 0)),
            ],
            scratch_shapes=[
                pltpu.VMEM((2, count, tasks, block, d), BF16),
                pltpu.SemaphoreType.DMA((2, count, tasks)),
            ],
        ),
        out_shape=[
            jax.ShapeDtypeStruct((local, rows, d), BF16),
            jax.ShapeDtypeStruct((rows, 2 * cols), BF16),
        ],
        **params(2**11 * rows * d, "spread_grads"),
    )(ids, *grads, gates, outs)


def backward_kernel(
    tasks, n, sub,
    ids_ref, og_ref, slope_ref, up_ref, down_ref, pair_ref, pg_ref, keep_ref, send_ref, acc_ref,
):
    e = pl.program_id(0)
    rows, d = acc_ref.shape
    for r in range(0, rows, sub):
        part = pl.ds(r, sub)
        hidden = mm(og_ref[0, part, :], down_ref[0], NT)
        pre_grad = (hidden * slope_ref[0, part, :].astype(F32)).astype(BF16)
        pg_ref[0, part, :] = pre_grad
        found = mm(pre_grad, up_ref[0], NT)

        @pl.when(e == 0)
        def _():
            acc_ref[part, :] = found

        @pl.when(e > 0)
        def _():
            acc_ref[part, :] += found

    block = rows // n
    quarter = block // tasks

    @pl.when(e == pl.num_programs(0) - 1)
    def _():
        for i in range(n):
            ref = keep_ref if i < n // 2 else send_ref
            for t in range(tasks):
                place = ids_ref[1 + 2 * tasks * i + tasks + t]
                begin = pl.multiple_of(i * block + place * quarter, quarter)
                source = pl.ds(begin, quarter)
                dest = pl.ds(i % (n // 2) * quarter, quarter)
                ref[t, dest, :d] = acc_ref[source, :].astype(BF16)
                ref[t, dest, d:] = pair_ref[source, :]


def backward(ids, og, slope, up, down, pair, n, tasks):
    local, rows, d = og.shape
    hid = up.shape[2]
    here = lambda e, f: (e, 0, 0)
    width = d + pair.shape[1]
    packed = (tasks, rows // 2 // tasks, width)
    return pl.pallas_call(
        functools.partial(backward_kernel, tasks, n, min(rows, 512)),
        grid_spec=pltpu.PrefetchScalarGridSpec(
            num_scalar_prefetch=1,
            grid=(local,),
            in_specs=[
                pl.BlockSpec((1, rows, d), here),
                pl.BlockSpec((1, rows, hid), here),
                pl.BlockSpec((1, d, hid), here),
                pl.BlockSpec((1, hid, d), here),
                pl.BlockSpec(pair.shape, lambda e, f: (0, 0)),
            ],
            out_specs=[pl.BlockSpec((1, rows, hid), here)]
            + [pl.BlockSpec(packed, lambda e, f: (0, 0, 0))] * 2,
            scratch_shapes=[pltpu.VMEM((rows, d), F32)],
        ),
        out_shape=[jax.ShapeDtypeStruct((local, rows, hid), BF16)]
        + [jax.ShapeDtypeStruct(packed, BF16)] * 2,
        **params(4 * rows * d * hid * local, "backward"),
    )(ids, og, slope, up, down, pair)


def weights_kernel(n, *refs):
    shared, acts, ogs, pgs = (refs[k * n : (k + 1) * n] for k in range(4))
    up_ref, down_ref = refs[-2:]
    total = sum(mm(s[...], p[0], TN) for s, p in zip(shared, pgs))
    up_ref[0] = total.astype(BF16)
    total = sum(mm(a[0], o[0], TN) for a, o in zip(acts, ogs))
    down_ref[0] = total.astype(BF16)


def weight_grads(shared, acts, ogs, pgs, begin, count, before):
    local, rows, hid = acts[0].shape
    d = shared[0].shape[1]
    n = len(shared)
    there = lambda e, h: (begin + e, 0, 0)
    half = [pl.BlockSpec((1, x.shape[1], hid // 2), lambda e, h: (begin + e, 0, h)) for x in acts]
    return pl.pallas_call(
        functools.partial(weights_kernel, n),
        grid=(count, 2),
        in_specs=[pl.BlockSpec(s.shape, lambda e, h: (0, 0)) for s in shared]
        + half
        + [pl.BlockSpec((1,) + x.shape[1:], there) for x in ogs]
        + half
        + [pl.BlockSpec(memory_space=pl.ANY) for _ in before],
        out_specs=[
            pl.BlockSpec((1, d, hid // 2), lambda e, h: (begin + e, 0, h)),
            pl.BlockSpec((1, hid // 2, d), lambda e, h: (begin + e, h, 0)),
        ],
        out_shape=[
            jax.ShapeDtypeStruct((local, d, hid), BF16),
            jax.ShapeDtypeStruct((local, hid, d), BF16),
        ],
        input_output_aliases={4 * n + k: k for k in range(len(before))},
        **params(4 * n * rows * d * hid * count, "weight_grads"),
    )(*shared, *acts, *ogs, *pgs, *before)


def rows_kernel(cols, every_ref, feat_ref, shared_ref, cross_ref, bias_ref, gating_ref, offset_ref):
    i = pl.program_id(0)
    d = feat_ref.shape[1]

    @pl.when(i == 0)
    def _():
        for ref in (cross_ref, bias_ref, gating_ref, offset_ref):
            ref[...] = jnp.zeros_like(ref)

    scaled = (every_ref[:, :d].astype(F32) * feat_ref[...].astype(F32)).astype(BF16)
    cross_ref[...] += mm(feat_ref[...], scaled, TN)
    bias_ref[...] += jnp.sum(scaled.astype(F32), axis=0, keepdims=True)
    pair = every_ref[:, d:]
    gating_ref[...] += mm(shared_ref[...], pair, TN)
    offset_ref[...] += jnp.sum(pair.astype(F32), axis=0, keepdims=True)


def rows_grads(every, feat, shared, cols):
    rows, d = feat.shape
    sub = min(rows, 512)
    width = every.shape[1]
    whole = lambda i: (0, 0)
    cross_grad, bias, gating, offset = pl.pallas_call(
        functools.partial(rows_kernel, cols),
        grid=(rows // sub,),
        in_specs=[
            pl.BlockSpec((sub, width), lambda i: (i, 0)),
            pl.BlockSpec((sub, d), lambda i: (i, 0)),
            pl.BlockSpec((sub, d), lambda i: (i, 0)),
        ],
        out_specs=[
            pl.BlockSpec((d, d), whole),
            pl.BlockSpec((1, d), whole),
            pl.BlockSpec((d, width - d), whole),
            pl.BlockSpec((1, width - d), whole),
        ],
        out_shape=[
            jax.ShapeDtypeStruct((d, d), F32),
            jax.ShapeDtypeStruct((1, d), F32),
            jax.ShapeDtypeStruct((d, width - d), F32),
            jax.ShapeDtypeStruct((1, width - d), F32),
        ],
        **params(2 * rows * d * d, "rows_grads"),
    )(every, feat, shared)
    return cross_grad, bias, gating[:, :cols], offset[0, :cols] + offset[0, cols:]


def added(parts):
    return sum(p.astype(F32) for p in parts)


class Ring:
    def __init__(self, dp, expert):
        size = dp * expert

        def pairs(move):
            found = []
            for i in range(size):
                z, c, q = i // expert // 2, i // expert % 2, i % expert
                z, c, q = move(z, c, q)
                found.append((i, (z * 2 + c) * expert + q))
            return found

        self.core_pairs = pairs(lambda z, c, q: (z, 1 - c, q))
        self.z1_pairs = pairs(lambda z, c, q: (z ^ 1, c, q))
        self.z3_pairs = pairs(lambda z, c, q: (z ^ 3, c, q))
        self.e1_pairs = pairs(lambda z, c, q: (z, c, q ^ (1, 2)[c]))
        self.e2_pairs = pairs(lambda z, c, q: (z, c, q ^ (2, 1)[c]))

    def move(self, x, pairs):
        return lax.ppermute(x, ("dp", "expert"), pairs)

    def core(self, x):
        return self.move(x, self.core_pairs)

    def orders(self):
        q, c = lax.axis_index("expert"), lax.axis_index("dp") % 2
        b1, b2 = 1 + c, 2 - c
        return [q, q ^ b2, q ^ b1, q ^ 3], [q, q ^ b1, q ^ b2, q ^ 3]

    def ids(self, first, tasks):
        mine, other = self.orders()
        plain = list(range(tasks))
        ids = [first]
        for order in (mine, other):
            for k in range(4):
                ids += plain if k == 0 else (other if order is mine else mine)
                ids += order
        return [jnp.stack([jnp.asarray(i, jnp.int32) for i in ids])]

    def spread(self, x):
        one = self.move(x, self.e1_pairs)
        rest = self.move(jnp.stack([x, one]), self.e2_pairs)
        return x[None], one[None], rest

    def in_order(self, parts, order):
        parts = jnp.concatenate(parts, axis=0)
        place = lambda share: sum(jnp.where(order[i] == share, i, 0) for i in range(4))
        return [lax.dynamic_index_in_dim(parts, place(i), 0, False) for i in range(4)]

    def rows(self, x):
        three = self.move(x, self.z3_pairs)
        mine = jnp.stack([x, three])
        rest = self.move(mine, self.z1_pairs)
        mine = jnp.concatenate([mine, rest], axis=0).reshape(-1, x.shape[-1])
        return [jnp.concatenate([mine, self.core(mine)], axis=0)], three, rest

    def grads(self, task_grad):
        own = jnp.transpose(task_grad, (1, 0, 2))
        share = lax.dynamic_index_in_dim(task_grad, lax.axis_index("expert"), 1, False)
        core, move = self.core, self.move
        share, own = yield (share, own)
        three, own2 = yield (move(share, self.z3_pairs), core(own))
        a0 = three[None]
        both, a0 = yield (jnp.stack([share, three]), a0)
        b0, a1 = yield (move(both, self.z1_pairs), move(a0, self.e1_pairs))
        b0, out = yield (b0, jnp.stack([a0, a1]))
        b1, a2 = yield (move(b0, self.e1_pairs), move(out, self.e2_pairs))
        out, *a = yield (jnp.stack([b0, b1]), a0, a1, a2)
        b2, *other_a = yield (move(out, self.e2_pairs), *map(core, a))
        b = yield (b0, b1, b2)
        other_b = yield tuple(map(core, b))
        lift = lambda x, y, z: [x[None], y[None], z]
        refs = [own, *lift(*a), *lift(*b), own2, *lift(*other_a), *lift(*other_b)]
        places = []
        for w in (0, 7):
            places.append(tuple((w, t) for t in range(4)))
            for k, j in ((1, 0), (4, 0), (4, 1)):
                places.append(
                    ((w + k, 0, j), (w + k + 1, 0, j), (w + k + 2, 0, j), (w + k + 2, 1, j))
                )
        return [(refs, tuple(places))]

    def reduce(self, parts, scatter):
        ((keep, send),) = parts
        (out,) = yield (send,)
        (got,) = yield (self.core(out),)
        parts = [keep, got]
        (out,) = yield (added([p[2:] for p in parts]).astype(BF16),)
        (got,) = yield (self.move(out, self.e1_pairs),)
        parts = [p[:2] for p in parts] + [got]
        (out,) = yield (added([p[1] for p in parts]).astype(BF16),)
        (got,) = yield (self.move(out, self.e2_pairs),)
        parts = [p[0] for p in parts] + [got]
        half = got.shape[0] // 2
        if scatter:
            (out,) = yield (added([p[half:] for p in parts]).astype(BF16),)
            (got,) = yield (self.move(out, self.z1_pairs),)
            parts = [p[:half] for p in parts] + [got]
            half = half // 2
            (out,) = yield (added([p[half:] for p in parts]).astype(BF16),)
            (got,) = yield (self.move(out, self.z3_pairs),)
            return added([p[:half] for p in parts] + [got])
        shape = (4, -1, got.shape[-1])
        (out,) = yield (added(parts).astype(BF16).reshape(shape),)
        (got,) = yield (self.move(out, self.z1_pairs),)
        out = added([out, jnp.concatenate([got[2:], got[:2]], axis=0)])
        (out,) = yield (out.astype(BF16),)
        (got,) = yield (self.move(out, self.z3_pairs),)
        return added([out, jnp.stack([got[1], got[0], got[3], got[2]])])

    def share_tasks(self, x):
        return self.in_order(self.spread(x), self.orders()[1])

    def share_rows(self, x):
        mine = self.spread(x)
        other = [self.core(p) for p in mine]
        rows = []
        for parts, order in zip((mine, other), self.orders()[::-1]):
            rows.append(jnp.stack(self.in_order(parts, order), axis=1).reshape(-1, x.shape[-1]))
        return jnp.concatenate(rows, axis=0)

    def own_rows(self, rows):
        return rows[: rows.shape[0] // 8]


class Steps:
    def __init__(self, steps):
        self.steps, self.moved, self.value = steps, None, None
        self.operand = self._next(None)

    def _next(self, sent):
        try:
            return self.steps.send(sent)
        except StopIteration as stop:
            self.value = stop.value

    def start(self, *after):
        if self.operand is not None:
            self.moved, self.operand = self._next(tie(self.operand, *after)), None

    def finish(self, *after):
        if self.moved is not None:
            moved, self.moved = self.moved, None
            self.operand = self._next(tie(moved, *after))

    def result(self):
        while self.moved is not None or self.operand is not None:
            self.start()
            self.finish()
        return self.value


def tie(x, *others):
    others = [o for o in others if o is not None]
    return lax.optimization_barrier((x, *others))[0] if others else x


class Plain:
    def __init__(self, dp, expert):
        self.dp = dp
        self.count = dp // 8 if dp % 8 == 0 else 1
        self.blocks = dp // self.count

    def ids(self, first, tasks):
        plain = list(range(tasks)) * 2 * self.blocks
        return [jnp.stack([jnp.asarray(i, jnp.int32) for i in (first, *plain)])] * self.count

    def rows(self, x):
        every = lax.all_gather(x, "dp", axis=0, tiled=True)
        return jnp.split(every, self.count), None, None

    def grads(self, task_grad):
        every = lax.all_gather(jnp.transpose(task_grad, (1, 0, 2)), "dp", axis=0)
        tasks = task_grad.shape[1]
        places = tuple(tuple((0, i, t) for t in range(tasks)) for i in range(self.blocks))
        return [([part], places) for part in jnp.split(every, self.count)]
        yield

    def reduce(self, parts, scatter):
        blocks = []
        for part in (p for pair in parts for p in pair):
            part = part.reshape(part.shape[0], self.blocks // 2, -1, part.shape[-1])
            blocks.append(jnp.swapaxes(part.astype(F32), 0, 1))
        blocks = jnp.concatenate(blocks, axis=0)
        own = lax.psum_scatter(blocks, "dp", scatter_dimension=0, tiled=True)[0]
        return lax.psum(own, "expert")
        yield

    def share_tasks(self, x):
        return list(x)

    def share_rows(self, x):
        every = lax.all_gather(x, "dp", axis=0)
        return every.reshape(-1, x.shape[-1])

    def own_rows(self, rows):
        n = rows.shape[0] // self.dp
        return lax.dynamic_slice_in_dim(rows, lax.axis_index("dp") * n, n, 0)


def local_step(
    net, features, cross_weight, cross_bias, gate_weight, gate_offset, up_weight, down_weight,
    task_grad,
):
    block, d = features.shape
    tasks = task_grad.shape[1]
    cols = gate_weight.shape[1]
    local = up_weight.shape[0]
    first = lax.axis_index("expert") * local
    ids = net.ids(first, tasks)
    step = max(local // FORWARD_PARTS, 1)

    feats, early, late = net.rows(features)
    grads = Steps(net.grads(task_grad))
    grads.start(early)

    lowered = [
        cross(f, cross_weight[0], cross_bias, gate_weight, gate_offset[None], tasks)
        for f in feats
    ]
    shared, gates = zip(*lowered)
    grads.finish(*shared)
    ready = grads.operand
    grads.start()
    done = [() for _ in shared]
    for b in range(0, local, step):
        if b:
            grads.finish(*[found[0] for found in done])
            ready = grads.operand
            grads.start()
        done = [
            forward(tie(low, ready), up_weight, down_weight, b, step, found)
            for low, found in zip(shared, done)
        ]
    acts, slopes, outs = zip(*done)
    grads.finish()
    grads = grads.result()
    lowered = [tie(gt, *g[0]) for gt, g in zip(gates, grads)]
    mixed = [mix(i, gt, o, len(g[1]), tasks) for i, gt, o, g in zip(ids, lowered, outs, grads)]
    mixed = Steps(net.reduce(mixed, True))
    mixed.start()
    spread = [
        spread_grads(i, *g, gt, o, tasks) for i, g, gt, o in zip(ids, grads, gates, outs)
    ]
    mixed.finish(*[og for og, _ in spread])
    ready = mixed.operand
    mixed.start()
    back = [
        backward(i, tie(og, ready), slope, up_weight, down_weight, pair, len(g[1]), tasks)
        for i, (og, pair), slope, g in zip(ids, spread, slopes, grads)
    ]
    ogs = [og for og, _ in spread]
    pgs = [b[0] for b in back]
    total = Steps(net.reduce([b[1:] for b in back], False))
    total.start()
    total.finish()
    mixed.finish(*pgs)
    weights = ()
    step = max(local // WEIGHT_PARTS, 1)
    for b in range(0, local, step):
        ready = (mixed.operand, total.operand)
        total.start()
        mixed.start()
        tied = [tie(a, *ready) for a in acts]
        weights = weight_grads(shared, tied, ogs, pgs, b, step, weights)
        total.finish(weights[0])
        mixed.finish(weights[0])
        total.start()
        total.finish()
    up_grad, down_grad = weights
    total = total.result()
    task_mixed = mixed.result().astype(BF16)
    task_mixed = jnp.stack(net.share_tasks(task_mixed), axis=1)

    logit = total[..., d : d + cols] + total[..., d + cols :]
    high = logit.astype(BF16)
    low = (logit - high.astype(F32)).astype(BF16)
    upstream = total[..., :d] + lax.dot_general(
        high, gate_weight, (((high.ndim - 1,), (1,)), ((), ())), preferred_element_type=F32
    )
    every = net.share_rows(jnp.concatenate([upstream.astype(BF16), high, low], axis=-1))

    cross_grad, bias_grad, gating_grad, offset_grad = rows_grads(
        every, jnp.concatenate(feats, axis=0), jnp.concatenate(shared, axis=0), cols
    )

    update = mm(features, cross_weight[0]) + cross_bias
    upstream = net.own_rows(every[:, :d]).astype(F32)
    scaled = (upstream * features.astype(F32)).astype(BF16)
    feature_grad = (upstream + mm(scaled, cross_weight[0], NT) + upstream * update).astype(BF16)
    return (
        task_mixed,
        feature_grad,
        up_grad,
        down_grad,
        cross_grad[None],
        bias_grad,
        gating_grad,
        offset_grad,
    )


def solution(mesh):
    dp, expert = mesh.shape["dp"], mesh.shape["expert"]
    net = (Ring if (dp, expert) == (8, 4) else Plain)(dp, expert)
    return jax.shard_map(
        functools.partial(local_step, net),
        mesh=mesh,
        in_specs=(
            P("dp", None),
            P(),
            P(),
            P(),
            P(),
            P("expert", None, "dp"),
            P("expert", "dp", None),
            P("dp", None, None),
        ),
        out_specs=(
            P("dp", None, None),
            P("dp", None),
            P("expert", None, "dp"),
            P("expert", "dp", None),
            P(),
            P(),
            P(),
            P(),
        ),
        check_vma=False,
    )
```

time: 611 us -> 276 us (0.45); the launches traced: 603 us -> 275 us
  waiting for transfers between devices: 410 us -> 69.6 us
  Pallas kernels: 0 us -> 133 us
  matrix products: 125 us -> 2.24 us
  starting transfers between devices: 0.67 us -> 38.1 us
  blocking collectives: 18.7 us -> 0 us
  local copies, waits for them, and re-layouts: 26 us -> 8.17 us
  other arithmetic: 7.36 us -> 22.6 us
  between operations: 14.7 us -> 1.1 us
    reduce_scatter x2 -> x0, waiting for transfers between devices: 166 us -> none  [the longest x1 133 us: local(): lax.psum_scatter(jnp.einsum('reh,ehd->red', hidden_act, down_weight, pref...]
    all_gather x3 -> x0, waiting for transfers between devices: 159 us -> none  [the longest x1 87.4 us: local(): all_out = lax.all_gather(group_out, 'expert', axis=1, tiled=True)]
    pallas_call x0 -> x12, Pallas kernels: none -> 133 us  [the longest x4 34.2 us: forward(): pl.pallas_call(forward_kernel, grid=(count, rows // sub), in_specs=[pl.Bl...]
    dot_general x13 -> x3, matrix products: 125 us -> 2.24 us  [the longest x2 2.04 us: mm(): return lax.dot_general(a, b, dims, preferred_element_type=F32)]
    psum x2 -> x0, waiting for transfers between devices: 84.6 us -> none  [the longest x1 42.6 us: local(): lax.psum((cross_part, bias_part, gating_part, offset_part), 'dp')]
    ppermute x0 -> x33, waiting for transfers between devices: none -> 69.6 us  [move(): return lax.ppermute(x, ('dp', 'expert'), pairs)]
    ppermute x0 -> x33, starting transfers between devices: none -> 38.1 us  [move(): return lax.ppermute(x, ('dp', 'expert'), pairs)]
    psum x1 -> x0, blocking collectives: 18.7 us -> none  [local(): lax.psum((cross_part, bias_part, gating_part, offset_part), 'dp')]
  transfers between devices with their start and end apart: 7 -> 33, of which waited for: 7 -> 12; matrix products, arithmetic and copies ran while one was open for 24% -> 8% of each run, Pallas kernels for 0% -> 44%
where the time goes in v1:
time: 276 us; the launch traced here: 275 us
  Pallas kernels  133 us (48%)
  waiting for transfers between devices  69.6 us (25%)
  starting transfers between devices  38.1 us (14%)
  other arithmetic  22.6 us (8%)
  local copies, waits for them, and re-layouts  8.17 us (3%)
    ppermute x33, waiting for transfers between devices, move(): return lax.ppermute(x, ('dp', 'expert'), pairs)  69.6 us
    ppermute x33, starting transfers between devices, move(): return lax.ppermute(x, ('dp', 'expert'), pairs)  38.1 us
    pallas_call x4, Pallas kernels, forward(): pl.pallas_call(forward_kernel, grid=(count, rows // sub), in_specs=[pl.Bl...  34.2 us
    pallas_call x2, Pallas kernels, weight_grads(): pl.pallas_call(functools.partial(weights_kernel, n), grid=(count, 2), in_...  27.6 us
    pallas_call x1, Pallas kernels, backward(): pl.pallas_call(functools.partial(backward_kernel, tasks, n, min(rows, 512...  27.5 us
    pallas_call x1, Pallas kernels, spread_grads(): pl.pallas_call(functools.partial(spread_kernel, tasks, cols // tasks, pla...  18.4 us
    pallas_call x2, Pallas kernels, half(): pl.pallas_call(functools.partial(mix_kernel, tasks, cols // tasks, rows /...  11.3 us
    pallas_call x1, Pallas kernels, rows_grads(): pl.pallas_call(functools.partial(rows_kernel, cols), grid=(rows // sub,),...  7.39 us
  transfers between devices with their start and end apart: 33, of which 12 were waited for; matrix products, arithmetic and copies ran while one was open for 8% of the time, Pallas kernels for 44%

profile of v1, /device:TPU:0, one launch (start us, length us, event | category | flops | bytes accessed | tf_op | source)
XLA Modules:
  0.0 275.2 jit_solution(16552881508069907472)
XLA Ops:
  0.6 5.1 %collective-permute-start = (bf16[128,1024]{1,0:T(8,128)(2,1)}, bf16[128,1024]{1,0:T(8,128)(2,1)S(1)}, u32[]{:S(2)}, u32[]{:S(2)}) collective-permute-start(bf16[128,1024]{1,0:T(8,128)(2,1)} %param.8), channel_id=1, source_target_pairs={{0,24},{1,25},{2,26},{3,27},{4,28},{5,29},{6,30},{7,31},{8,16},{9,... | collective-permute-start | bytes 786440 | tf_op jit(solution)/shard_map/ppermute | solution.py:477
  5.8 6.6 %collective-permute-done = bf16[128,1024]{1,0:T(8,128)(2,1)S(1)} collective-permute-done((bf16[128,1024]{1,0:T(8,128)(2,1)}, bf16[128,1024]{1,0:T(8,128)(2,1)S(1)}, u32[]{:S(2)}, u32[]{:S(2)}) %collective-permute-start) | collective-permute-done | bytes 262176 | tf_op jit(solution)/shard_map/ppermute | solution.py:477
  13.4 5.3 %collective-permute-start.1 = (bf16[2,128,1024]{2,1,0:T(8,128)(2,1)S(1)}, bf16[2,128,1024]{2,1,0:T(8,128)(2,1)S(1)}, u32[]{:S(2)}, u32[]{:S(2)}) collective-permute-start(bf16[2,128,1024]{2,1,0:T(8,128)(2,1)S(1)} %pad_maximum_fusion.10), channel_id=1, source_target_pairs={{0,8},{1,9},{2,10},{3,11},{4,12},{5,13},{6,14},{7,15},{8,0},{9,1},... | collective-permute-start | bytes 1572872 | tf_op jit(solution)/shard_map/ppermute | solution.py:477
  18.7 11.2 %collective-permute-done.1 = bf16[2,128,1024]{2,1,0:T(8,128)(2,1)S(1)} collective-permute-done((bf16[2,128,1024]{2,1,0:T(8,128)(2,1)S(1)}, bf16[2,128,1024]{2,1,0:T(8,128)(2,1)S(1)}, u32[]{:S(2)}, u32[]{:S(2)}) %collective-permute-start.1) | collective-permute-done | bytes 524320 | tf_op jit(solution)/shard_map/ppermute | solution.py:477
  38.5 6.9 %cross.1 = (bf16[1024,1024]{1,0:T(8,128)(2,1)}, f32[1024,64]{1,0:T(8,128)}) custom-call(bf16[1024,1024]{1,0:T(8,128)(2,1)} %pad_maximum_fusion.1.feat_ref, bf16[1024,1024]{1,0:T(8,128)(2,1)} %bitcast.96, f32[1,1024]{1,0:T(1,128)} %cb_ref.1, bf16[1024,64]{1,0:T(8,128)(2,1)} %copy.30.gw_ref, f32[1,64]{1,0:T(1,128)} %bitcast.137), custom_call_target="tpu_custom_call" | custom-call | flops 2147483648 | bytes 4194304 | tf_op jit(solution)/shard_map/cross/pallas_call | solution.py:67
  45.5 3.9 %collective-permute-start.5 = (bf16[2,128,1024]{2,1,0:T(8,128)(2,1)S(1)}, bf16[2,128,1024]{2,1,0:T(8,128)(2,1)S(1)}, u32[]{:S(2)}, u32[]{:S(2)}) collective-permute-start(bf16[2,128,1024]{2,1,0:T(8,128)(2,1)S(1)} %pad_maximum_fusion.11), channel_id=1, source_target_pairs={{0,8},{1,9},{2,10},{3,11},{4,12},{5,13},{6,14},{7,15},{8,0},{9,1},... | collective-permute-start | bytes 1572872 | tf_op jit(solution)/shard_map/ppermute | solution.py:477
  50.9 8.5 %forward.4 = (bf16[4,1024,1024]{2,1,0:T(8,128)(2,1)}, bf16[4,1024,1024]{2,1,0:T(8,128)(2,1)}, bf16[4,1024,1024]{2,1,0:T(8,128)(2,1)}) custom-call(bf16[1024,1024]{1,0:T(8,128)(2,1)} %get-tuple-element.86.shared_ref.refs_0_, bf16[4,1024,1024]{2,1,0:T(8,128)(2,1)} %up_ref.9, bf16[4,1024,1024]{2,1,0:T(8,128)(2,1)} %down_ref.9), custom_call_target="tpu_custom_call" | custom-call | flops 4294967296 | bytes 4194304 | tf_op jit(solution)/shard_map/forward/pallas_call | solution.py:107
  64.1 8.6 %forward.5 = (bf16[4,1024,1024]{2,1,0:T(8,128)(2,1)}, bf16[4,1024,1024]{2,1,0:T(8,128)(2,1)}, bf16[4,1024,1024]{2,1,0:T(8,128)(2,1)}) custom-call(bf16[1024,1024]{1,0:T(8,128)(2,1)} %get-tuple-element.86.shared_ref.refs_0_, bf16[4,1024,1024]{2,1,0:T(8,128)(2,1)} %up_ref.9, ...), custom_call_target="tpu_custom_call", output_to_operand_aliasing={{0}: (3, {}), {1}: (4, {}), {2}: (5, {})} | custom-call | flops 4294967296 | bytes 4194304 | tf_op jit(solution)/shard_map/forward/pallas_call | solution.py:107
  77.2 8.6 %forward.6 = (bf16[4,1024,1024]{2,1,0:T(8,128)(2,1)}, bf16[4,1024,1024]{2,1,0:T(8,128)(2,1)}, bf16[4,1024,1024]{2,1,0:T(8,128)(2,1)}) custom-call(bf16[1024,1024]{1,0:T(8,128)(2,1)} %get-tuple-element.86.shared_ref.refs_0_, bf16[4,1024,1024]{2,1,0:T(8,128)(2,1)} %up_ref.9, ...), custom_call_target="tpu_custom_call", output_to_operand_aliasing={{0}: (3, {}), {1}: (4, {}), {2}: (5, {})} | custom-call | flops 4294967296 | bytes 4194304 | tf_op jit(solution)/shard_map/forward/pallas_call | solution.py:107
  85.8 4.1 %collective-permute-done.9.refs_6_ = bf16[2,2,128,1024]{3,2,1,0:T(8,128)(2,1)S(1)} collective-permute-done((bf16[2,2,128,1024]{3,2,1,0:T(8,128)(2,1)S(1)}, bf16[2,2,128,1024]{3,2,1,0:T(8,128)(2,1)S(1)}, u32[]{:S(2)}, u32[]{:S(2)}) %collective-permute-start.9) | collective-permute-done | bytes 1048608 | tf_op jit(solution)/shard_map/ppermute | solution.py:477
  91.2 8.5 %forward.7 = (bf16[4,1024,1024]{2,1,0:T(8,128)(2,1)}, bf16[4,1024,1024]{2,1,0:T(8,128)(2,1)}, bf16[4,1024,1024]{2,1,0:T(8,128)(2,1)}) custom-call(bf16[1024,1024]{1,0:T(8,128)(2,1)} %get-tuple-element.86.shared_ref.refs_0_, bf16[4,1024,1024]{2,1,0:T(8,128)(2,1)} %up_ref.9, ...), custom_call_target="tpu_custom_call", output_to_operand_aliasing={{0}: (3, {}), {1}: (4, {}), {2}: (5, {})} | custom-call | flops 4294967296 | bytes 4194304 | tf_op jit(solution)/shard_map/forward/pallas_call | solution.py:107
  99.8 5.7 %mix.3 = bf16[4,512,1024]{2,1,0:T(8,128)(2,1)} custom-call(s32[65]{0:T(128)} %stack.69.ids_ref, f32[1024,64]{1,0:T(8,128)} %get-tuple-element.85.gates_ref.refs_14_, bf16[4,1024,1024]{2,1,0:T(8,128)(2,1)} %get-tuple-element.89.outs_ref.refs_15_), custom_call_target="tpu_custom_call" | custom-call | flops 1073741824 | bytes 4194304 | tf_op jit(solution)/shard_map/mix/pallas_call | solution.py:179
  105.9 5.7 %mix.2 = bf16[4,512,1024]{2,1,0:T(8,128)(2,1)} custom-call(s32[65]{0:T(128)} %stack.69.ids_ref, f32[1024,64]{1,0:T(8,128)} %get-tuple-element.85.gates_ref.refs_14_, bf16[4,1024,1024]{2,1,0:T(8,128)(2,1)} %get-tuple-element.89.outs_ref.refs_15_), custom_call_target="tpu_custom_call" | custom-call | flops 1073741824 | bytes 4194304 | tf_op jit(solution)/shard_map/mix/pallas_call | solution.py:179
  111.5 18.4 %spread_grads.1 = (bf16[4,1024,1024]{2,1,0:T(8,128)(2,1)}, bf16[1024,128]{1,0:T(8,128)(2,1)}) custom-call(s32[65]{0:T(128)} %stack.69.ids_ref, bf16[4,128,1024]{2,1,0:T(8,128)(2,1)} %bitcast.101, bf16[1,1,128,1024]{3,2,1,0:T(8,128)(2,1)} %bitcast.114, bf16[1,1,128,1024]{3,2,1,0:T(8,128)(2,1)} %bitcast.127, bf16[2,1,128,1024]{3,2,1,0:T(8,128)(2,1)} %copy-done.14, ...), custom_call_target="tpu_custom_call" | custom-call | flops 2147483648 | bytes 4194304 | tf_op jit(solution)/shard_map/spread_grads/pallas_call | solution.py:279
  133.2 27.5 %backward.1 = (bf16[4,1024,1024]{2,1,0:T(8,128)(2,1)}, bf16[4,128,1152]{2,1,0:T(8,128)(2,1)}, bf16[4,128,1152]{2,1,0:T(8,128)(2,1)}) custom-call(s32[65]{0:T(128)} %stack.69.ids_ref, bf16[4,1024,1024]{2,1,0:T(8,128)(2,1)} %get-tuple-element.92.og_ref.refs_2_, bf16[4,1024,1024]{2,1,0:T(8,128)(2,1)} %get-tuple-element.93.slope_ref, ...), custom_call_target="tpu_custom_call" | custom-call | flops 17179869184 | bytes 4194304 | tf_op jit(solution)/shard_map/backward/pallas_call | solution.py:349
  171.2 13.7 %weight_grads.2 = (bf16[4,1024,1024]{2,1,0:T(8,128)(2,1)}, bf16[4,1024,1024]{2,1,0:T(8,128)(2,1)}) custom-call(bf16[1024,1024]{1,0:T(8,128)(2,1)} %get-tuple-element.86.shared_ref.refs_0_, bf16[4,1024,1024]{2,1,0:T(8,128)(2,1)} %get-tuple-element.104.refs_1_, bf16[4,1024,1024]{2,1,0:T(8,128)(2,1)} %get-tuple-element.92.og_ref.refs_2_, ...), custom_call_target="tpu_custom_call" | custom-call | flops 8589934592 | bytes 4194304 | tf_op jit(solution)/shard_map/weight_grads/pallas_call | solution.py:386
  186.6 6.2 %collective-permute-done.22 = bf16[128,1152]{1,0:T(8,128)(2,1)S(1)} collective-permute-done((bf16[128,1152]{1,0:T(8,128)(2,1)S(1)}, bf16[128,1152]{1,0:T(8,128)(2,1)S(1)}, u32[]{:S(2)}, u32[]{:S(2)}) %collective-permute-start.22) | collective-permute-done | bytes 294944 | tf_op jit(solution)/shard_map/ppermute | solution.py:477
  197.1 13.9 %weight_grads.3 = (bf16[4,1024,1024]{2,1,0:T(8,128)(2,1)}, bf16[4,1024,1024]{2,1,0:T(8,128)(2,1)}) custom-call(bf16[1024,1024]{1,0:T(8,128)(2,1)} %get-tuple-element.86.shared_ref.refs_0_, bf16[4,1024,1024]{2,1,0:T(8,128)(2,1)} %get-tuple-element.104.refs_1_, ...), custom_call_target="tpu_custom_call", output_to_operand_aliasing={{0}: (4, {}), {1}: (5, {})} | custom-call | flops 8589934592 | bytes 4194304 | tf_op jit(solution)/shard_map/weight_grads/pallas_call | solution.py:386
  213.5 9.5 %collective-permute-done.27 = bf16[4,32,1152]{2,1,0:T(8,128)(2,1)S(1)} collective-permute-done((bf16[4,32,1152]{2,1,0:T(8,128)(2,1)S(1)}, bf16[4,32,1152]{2,1,0:T(8,128)(2,1)S(1)}, u32[]{:S(2)}, u32[]{:S(2)}) %collective-permute-start.27) | collective-permute-done | bytes 294944 | tf_op jit(solution)/shard_map/ppermute | solution.py:477
  224.1 7.5 %collective-permute-done.20 = bf16[256,1024]{1,0:T(8,128)(2,1)S(1)} collective-permute-done((bf16[256,1024]{1,0:T(8,128)(2,1)S(1)}, bf16[256,1024]{1,0:T(8,128)(2,1)S(1)}, u32[]{:S(2)}, u32[]{:S(2)}) %collective-permute-start.20) | collective-permute-done | bytes 524320 | tf_op jit(solution)/shard_map/ppermute | solution.py:477
  235.9 7.3 %collective-permute-done.23 = bf16[128,1024]{1,0:T(8,128)(2,1)S(1)} collective-permute-done((bf16[128,1024]{1,0:T(8,128)(2,1)S(1)}, bf16[128,1024]{1,0:T(8,128)(2,1)S(1)}, u32[]{:S(2)}, u32[]{:S(2)}) %collective-permute-start.23) | collective-permute-done | bytes 262176 | tf_op jit(solution)/shard_map/ppermute | solution.py:477
  245.4 5.7 %collective-permute-done.24 = bf16[128,1024]{1,0:T(8,128)(2,1)S(1)} collective-permute-done((bf16[128,1024]{1,0:T(8,128)(2,1)S(1)}, bf16[128,1024]{1,0:T(8,128)(2,1)S(1)}, u32[]{:S(2)}, u32[]{:S(2)}) %collective-permute-start.24) | collective-permute-done | bytes 262176 | tf_op jit(solution)/shard_map/ppermute | solution.py:477
  255.6 4.9 %collective-permute-done.25 = bf16[2,128,1024]{2,1,0:T(8,128)(2,1)S(1)} collective-permute-done((bf16[2,128,1024]{2,1,0:T(8,128)(2,1)S(1)}, bf16[2,128,1024]{2,1,0:T(8,128)(2,1)S(1)}, u32[]{:S(2)}, u32[]{:S(2)}) %collective-permute-start.25) | collective-permute-done | bytes 524320 | tf_op jit(solution)/shard_map/ppermute | solution.py:477
  264.6 7.4 %rows_grads.1 = (f32[1024,1024]{1,0:T(8,128)}, f32[1,1024]{1,0:T(1,128)}, f32[1024,128]{1,0:T(8,128)}, f32[1,128]{1,0:T(1,128)}) custom-call(bf16[1024,1152]{1,0:T(8,128)(2,1)} %pad_maximum_fusion.every_ref, bf16[1024,1024]{1,0:T(8,128)(2,1)} %pad_maximum_fusion.1.feat_ref, bf16[1024,1024]{1,0:T(8,128)(2,1)} %get-tuple-element.86.shared_ref.refs_0_), custom_call_target="tpu_custom_call" | custom-call | flops 2147483648 | bytes 4194304 | tf_op jit(solution)/shard_map/rows_grads/pallas_call | solution.py:429
  (138 shorter events, 63.2 us)
Async XLA Ops:
  0.6 11.7 %collective-permute-start = (bf16[128,1024]{1,0:T(8,128)(2,1)}, bf16[128,1024]{1,0:T(8,128)(2,1)S(1)}, u32[]{:S(2)}, u32[]{:S(2)}) collective-permute-start(bf16[128,1024]{1,0:T(8,128)(2,1)} %param.8), channel_id=1, source_target_pairs={{0,24},{1,25},{2,26},{3,27},{4,28},{5,29},{6,30},{7,31},{8,16},{9,... | collective-permute-start | bytes 786440 | tf_op jit(solution)/shard_map/ppermute | solution.py:477
  13.4 16.5 %collective-permute-start.1 = (bf16[2,128,1024]{2,1,0:T(8,128)(2,1)S(1)}, bf16[2,128,1024]{2,1,0:T(8,128)(2,1)S(1)}, u32[]{:S(2)}, u32[]{:S(2)}) collective-permute-start(bf16[2,128,1024]{2,1,0:T(8,128)(2,1)S(1)} %pad_maximum_fusion.10), channel_id=1, source_target_pairs={{0,8},{1,9},{2,10},{3,11},{4,12},{5,13},{6,14},{7,15},{8,0},{9,1},... | collective-permute-start | bytes 1572872 | tf_op jit(solution)/shard_map/ppermute | solution.py:477
  32.2 13.3 %collective-permute-start.4 = (bf16[4,128,1024]{2,1,0:T(8,128)(2,1)S(1)}, bf16[4,128,1024]{2,1,0:T(8,128)(2,1)S(1)}, u32[]{:S(2)}, u32[]{:S(2)}) collective-permute-start(bf16[4,128,1024]{2,1,0:T(8,128)(2,1)S(1)} %bitcast.100), channel_id=1, source_target_pairs={{0,4},{1,5},{2,6},{3,7},{4,0},{5,1},{6,2},{7,3},{8,12},{9,13},{10,... | collective-permute-start | bytes 3145736 | tf_op jit(solution)/shard_map/ppermute | solution.py:477
  33.5 11.9 %collective-permute-start.3 = (bf16[128,1024]{1,0:T(8,128)(2,1)}, bf16[128,1024]{1,0:T(8,128)(2,1)S(1)}, u32[]{:S(2)}, u32[]{:S(2)}) collective-permute-start(bf16[128,1024]{1,0:T(8,128)(2,1)} %dynamic-slice_bitcast_fusion.12), channel_id=1, source_target_pairs={{0,24},{1,25},{2,26},{3,27},{4,28},{5,29},{6,30},{7,31},{8,16},{9,... | collective-permute-start | bytes 786440 | tf_op jit(solution)/shard_map/ppermute | solution.py:477
  45.5 15.4 %collective-permute-start.5 = (bf16[2,128,1024]{2,1,0:T(8,128)(2,1)S(1)}, bf16[2,128,1024]{2,1,0:T(8,128)(2,1)S(1)}, u32[]{:S(2)}, u32[]{:S(2)}) collective-permute-start(bf16[2,128,1024]{2,1,0:T(8,128)(2,1)S(1)} %pad_maximum_fusion.11), channel_id=1, source_target_pairs={{0,8},{1,9},{2,10},{3,11},{4,12},{5,13},{6,14},{7,15},{8,0},{9,1},... | collective-permute-start | bytes 1572872 | tf_op jit(solution)/shard_map/ppermute | solution.py:477
  49.5 10.0 %collective-permute-start.6 = (bf16[1,128,1024]{2,1,0:T(8,128)(2,1)S(1)}, bf16[1,128,1024]{2,1,0:T(8,128)(2,1)S(1)}, u32[]{:S(2)}, u32[]{:S(2)}) collective-permute-start(bf16[1,128,1024]{2,1,0:T(8,128)(2,1)S(1)} %bitcast.111), channel_id=1, source_target_pairs={{0,1},{1,0},{2,3},{3,2},{4,6},{5,7},{6,4},{7,5},{8,9},{9,8},{10,11... | collective-permute-start | bytes 786440 | tf_op jit(solution)/shard_map/ppermute | solution.py:477
  61.0 13.9 %collective-permute-start.8 = (bf16[2,1,128,1024]{3,2,1,0:T(8,128)(2,1)S(1)}, bf16[2,1,128,1024]{3,2,1,0:T(8,128)(2,1)S(1)}, u32[]{:S(2)}, u32[]{:S(2)}) collective-permute-start(bf16[2,1,128,1024]{3,2,1,0:T(8,128)(2,1)S(1)} %pad_maximum_fusion.12), channel_id=1, source_target_pairs={{0,2},{1,3},{2,0},{3,1},{4,5},{5,4},{6,7},{7,6},{8,10},{9,11},{10,... | collective-permute-start | bytes 1572872 | tf_op jit(solution)/shard_map/ppermute | solution.py:477
  62.6 12.3 %collective-permute-start.7 = (bf16[2,128,1024]{2,1,0:T(8,128)(2,1)S(1)}, bf16[2,128,1024]{2,1,0:T(8,128)(2,1)S(1)}, u32[]{:S(2)}, u32[]{:S(2)}) collective-permute-start(bf16[2,128,1024]{2,1,0:T(8,128)(2,1)S(1)} %collective-permute-done.5), channel_id=1, source_target_pairs={{0,1},{1,0},{2,3},{3,2},{4,6},{5,7},{6,4},{7,5},{8,9},{9,8},{10,11... | collective-permute-start | bytes 1572872 | tf_op jit(solution)/shard_map/ppermute | solution.py:477
  75.0 14.9 %collective-permute-start.9 = (bf16[2,2,128,1024]{3,2,1,0:T(8,128)(2,1)S(1)}, bf16[2,2,128,1024]{3,2,1,0:T(8,128)(2,1)S(1)}, u32[]{:S(2)}, u32[]{:S(2)}) collective-permute-start(bf16[2,2,128,1024]{3,2,1,0:T(8,128)(2,1)S(1)} %pad_maximum_fusion.6), channel_id=1, source_target_pairs={{0,2},{1,3},{2,0},{3,1},{4,5},{5,4},{6,7},{7,6},{8,10},{9,11},{10,... | collective-permute-start | bytes 3145736 | tf_op jit(solution)/shard_map/ppermute | solution.py:477
  89.9 9.9 %collective-permute-start.15 = (bf16[2,2,128,1024]{3,2,1,0:T(8,128)(2,1)S(1)}, bf16[2,2,128,1024]{3,2,1,0:T(8,128)(2,1)S(1)}, u32[]{:S(2)}, u32[]{:S(2)}) collective-permute-start(bf16[2,2,128,1024]{3,2,1,0:T(8,128)(2,1)S(1)} %collective-permute-done.9.refs_6_), channel_id=1, source_target_pairs={{0,4},{1,5},{2,6},{3,7},{4,0},{5,1},{6,2},{7,3},{8,12},{9,13},{10,... | collective-permute-start | bytes 3145736 | tf_op jit(solution)/shard_map/ppermute | solution.py:477
  89.9 9.8 %collective-permute-start.13 = (bf16[2,128,1024]{2,1,0:T(8,128)(2,1)S(1)}, bf16[2,128,1024]{2,1,0:T(8,128)(2,1)}, u32[]{:S(2)}, u32[]{:S(2)}) collective-permute-start(bf16[2,128,1024]{2,1,0:T(8,128)(2,1)S(1)} %collective-permute-done.5), channel_id=1, source_target_pairs={{0,4},{1,5},{2,6},{3,7},{4,0},{5,1},{6,2},{7,3},{8,12},{9,13},{10,... | collective-permute-start | bytes 1572872 | tf_op jit(solution)/shard_map/ppermute | solution.py:477
  105.5 24.5 %collective-permute-start.16 = (bf16[4,512,1024]{2,1,0:T(8,128)(2,1)}, bf16[4,512,1024]{2,1,0:T(8,128)(2,1)}, u32[]{:S(2)}, u32[]{:S(2)}) collective-permute-start(bf16[4,512,1024]{2,1,0:T(8,128)(2,1)} %mix.3), channel_id=1, source_target_pairs={{0,4},{1,5},{2,6},{3,7},{4,0},{5,1},{6,2},{7,3},{8,12},{9,13},{10,... | collective-permute-start | bytes 12582920 | tf_op jit(solution)/shard_map/ppermute | solution.py:477
  132.6 34.0 %collective-permute-start.17 = (bf16[2,512,1024]{2,1,0:T(8,128)(2,1)S(1)}, bf16[2,512,1024]{2,1,0:T(8,128)(2,1)}, u32[]{:S(2)}, u32[]{:S(2)}) collective-permute-start(bf16[2,512,1024]{2,1,0:T(8,128)(2,1)S(1)} %add_convert_fusion), channel_id=1, source_target_pairs={{0,1},{1,0},{2,3},{3,2},{4,6},{5,7},{6,4},{7,5},{8,9},{9,8},{10,11... | collective-permute-start | bytes 6291464 | tf_op jit(solution)/shard_map/ppermute | solution.py:477
  165.4 19.5 %collective-permute-start.21 = (bf16[2,128,1152]{2,1,0:T(8,128)(2,1)S(1)}, bf16[2,128,1152]{2,1,0:T(8,128)(2,1)}, u32[]{:S(2)}, u32[]{:S(2)}) collective-permute-start(bf16[2,128,1152]{2,1,0:T(8,128)(2,1)S(1)} %add_convert_fusion.2), channel_id=1, source_target_pairs={{0,1},{1,0},{2,3},{3,2},{4,6},{5,7},{6,4},{7,5},{8,9},{9,8},{10,11... | collective-permute-start | bytes 1769480 | tf_op jit(solution)/shard_map/ppermute | solution.py:477
  169.7 25.7 %collective-permute-start.18 = (bf16[512,1024]{1,0:T(8,128)(2,1)}, bf16[512,1024]{1,0:T(8,128)(2,1)}, u32[]{:S(2)}, u32[]{:S(2)}) collective-permute-start(bf16[512,1024]{1,0:T(8,128)(2,1)} %fusion.4), channel_id=1, source_target_pairs={{0,2},{1,3},{2,0},{3,1},{4,5},{5,4},{6,7},{7,6},{8,10},{9,11},{10,... | collective-permute-start | bytes 3145736 | tf_op jit(solution)/shard_map/ppermute | solution.py:477
  193.9 17.1 %collective-permute-start.26 = (bf16[4,32,1152]{2,1,0:T(8,128)(2,1)S(1)}, bf16[4,32,1152]{2,1,0:T(8,128)(2,1)S(1)}, u32[]{:S(2)}, u32[]{:S(2)}) collective-permute-start(bf16[4,32,1152]{2,1,0:T(8,128)(2,1)S(1)} %bitcast.124), channel_id=1, source_target_pairs={{0,8},{1,9},{2,10},{3,11},{4,12},{5,13},{6,14},{7,15},{8,0},{9,1},... | collective-permute-start | bytes 884744 | tf_op jit(solution)/shard_map/ppermute | solution.py:477
  211.1 11.9 %collective-permute-start.27 = (bf16[4,32,1152]{2,1,0:T(8,128)(2,1)S(1)}, bf16[4,32,1152]{2,1,0:T(8,128)(2,1)S(1)}, u32[]{:S(2)}, u32[]{:S(2)}) collective-permute-start(bf16[4,32,1152]{2,1,0:T(8,128)(2,1)S(1)} %add_convert_fusion.3), channel_id=1, source_target_pairs={{0,24},{1,25},{2,26},{3,27},{4,28},{5,29},{6,30},{7,31},{8,16},{9,... | collective-permute-start | bytes 884744 | tf_op jit(solution)/shard_map/ppermute | solution.py:477
  213.5 18.2 %collective-permute-start.20 = (bf16[256,1024]{1,0:T(8,128)(2,1)S(1)}, bf16[256,1024]{1,0:T(8,128)(2,1)S(1)}, u32[]{:S(2)}, u32[]{:S(2)}) collective-permute-start(bf16[256,1024]{1,0:T(8,128)(2,1)S(1)} %fusion.5), channel_id=1, source_target_pairs={{0,8},{1,9},{2,10},{3,11},{4,12},{5,13},{6,14},{7,15},{8,0},{9,1},... | collective-permute-start | bytes 1572872 | tf_op jit(solution)/shard_map/ppermute | solution.py:477
  223.5 11.3 %collective-permute-start.28 = (bf16[4,32,1152]{2,1,0:T(8,128)(2,1)S(1)}, bf16[4,32,1152]{2,1,0:T(8,128)(2,1)S(1)}, u32[]{:S(2)}, u32[]{:S(2)}) collective-permute-start(bf16[4,32,1152]{2,1,0:T(8,128)(2,1)S(1)} %concatenate.29), channel_id=1, source_target_pairs={{0,1},{1,0},{2,3},{3,2},{4,6},{5,7},{6,4},{7,5},{8,9},{9,8},{10,11... | collective-permute-start | bytes 884744 | tf_op jit(solution)/shard_map/ppermute | solution.py:477
  233.1 10.2 %collective-permute-start.23 = (bf16[128,1024]{1,0:T(8,128)(2,1)S(1)}, bf16[128,1024]{1,0:T(8,128)(2,1)S(1)}, u32[]{:S(2)}, u32[]{:S(2)}) collective-permute-start(bf16[128,1024]{1,0:T(8,128)(2,1)S(1)} %fusion.9), channel_id=1, source_target_pairs={{0,24},{1,25},{2,26},{3,27},{4,28},{5,29},{6,30},{7,31},{8,16},{9,... | collective-permute-start | bytes 786440 | tf_op jit(solution)/shard_map/ppermute | solution.py:477
  234.8 10.6 %collective-permute-start.30 = (bf16[1,4,32,1152]{3,2,1,0:T(8,128)(2,1)S(1)}, bf16[1,4,32,1152]{3,2,1,0:T(8,128)(2,1)S(1)}, u32[]{:S(2)}, u32[]{:S(2)}) collective-permute-start(bf16[1,4,32,1152]{3,2,1,0:T(8,128)(2,1)S(1)} %bitcast.107), channel_id=1, source_target_pairs={{0,4},{1,5},{2,6},{3,7},{4,0},{5,1},{6,2},{7,3},{8,12},{9,13},{10,... | collective-permute-start | bytes 884744 | tf_op jit(solution)/shard_map/ppermute | solution.py:477
  234.8 10.6 %collective-permute-start.31 = (bf16[1,4,32,1152]{3,2,1,0:T(8,128)(2,1)S(1)}, bf16[1,4,32,1152]{3,2,1,0:T(8,128)(2,1)S(1)}, u32[]{:S(2)}, u32[]{:S(2)}) collective-permute-start(bf16[1,4,32,1152]{3,2,1,0:T(8,128)(2,1)S(1)} %bitcast.121), channel_id=1, source_target_pairs={{0,4},{1,5},{2,6},{3,7},{4,0},{5,1},{6,2},{7,3},{8,12},{9,13},{10,... | collective-permute-start | bytes 884744 | tf_op jit(solution)/shard_map/ppermute | solution.py:477
  235.4 16.4 %collective-permute-start.29 = (bf16[2,4,32,1152]{3,2,1,0:T(8,128)(2,1)S(1)}, bf16[2,4,32,1152]{3,2,1,0:T(8,128)(2,1)S(1)}, u32[]{:S(2)}, u32[]{:S(2)}) collective-permute-start(bf16[2,4,32,1152]{3,2,1,0:T(8,128)(2,1)S(1)} %pad_maximum_fusion.9), channel_id=1, source_target_pairs={{0,2},{1,3},{2,0},{3,1},{4,5},{5,4},{6,7},{7,6},{8,10},{9,11},{10,... | collective-permute-start | bytes 1769480 | tf_op jit(solution)/shard_map/ppermute | solution.py:477
  252.3 10.3 %collective-permute-start.32 = (bf16[2,4,32,1152]{3,2,1,0:T(8,128)(2,1)S(1)}, bf16[2,4,32,1152]{3,2,1,0:T(8,128)(2,1)S(1)}, u32[]{:S(2)}, u32[]{:S(2)}) collective-permute-start(bf16[2,4,32,1152]{3,2,1,0:T(8,128)(2,1)S(1)} %collective-permute-done.29), channel_id=1, source_target_pairs={{0,4},{1,5},{2,6},{3,7},{4,0},{5,1},{6,2},{7,3},{8,12},{9,13},{10,... | collective-permute-start | bytes 1769480 | tf_op jit(solution)/shard_map/ppermute | solution.py:477
  (29 other events, 315.4 us)
